TPU v7x, 32 devices: a whole 2x2x4 slice. The times are simulated.
32 devices in a mesh: groups: 2 (over y), rows: 4 (over z), tm: 2 (over x), dp: 2 (over core).
Axes of the slice: x: 2, y: 2, z: 4, core: 2. Of those that a mesh axis runs over, the one named last changes fastest.
Arguments:
- frames_in: bfloat16 [4, 4, 16, 320, 128], P(('groups', 'dp'), 'tm', 'rows'), parts along dimension 0, may hold values from -6 to 6
- gain: float32 [128], replicated, may hold values from 0.5 to 1.5
- spatial_w: bfloat16 [3, 3, 128, 128], replicated, may hold values from -0.1875 to 0.1875
- temporal_w: bfloat16 [3, 128, 128], replicated, may hold values from -0.3125 to 0.3125
- cotangent: bfloat16 [4, 4, 16, 320, 128], P(('groups', 'dp'), 'tm', 'rows'), parts along dimension 0, may hold values from -6 to 6
Outputs:
- block_out: bfloat16 [4, 4, 16, 320, 128], P(('groups', 'dp'), 'tm', 'rows'), parts along dimension 0
- grad_input: bfloat16 [4, 4, 16, 320, 128], P(('groups', 'dp'), 'tm', 'rows'), parts along dimension 0
- grad_spatial: float32 [6, 3, 128, 128], P('groups'), parts along dimension 0
- grad_temporal: float32 [6, 128, 128], P('groups'), parts along dimension 0
- grad_gain: float32 [256], P('groups'), parts along dimension 0
There are 2 independent parts, one for each index of `groups`. A program takes and returns all parts, laid end to end along the dimension named above; an argument that names none is the same for every part. Nothing has to cross between parts.
All inputs are finite; a program needn't handle non-finite values.
Results may differ from a plain program's by a relative error of at most 0.0054.
Values may be sent and summed in bfloat16 or wider, within the bound.
A program may use at most 64 MiB of HBM per device.

v0:
```python
import math
import jax
import jax.numpy as jnp
from jax import lax
from jax.sharding import PartitionSpec as P

EPS = 1e-06


def extended(shard, sides, width):
    for axis, dim in sides:
        size, length = (lax.axis_size(axis), shard.shape[dim])
        up = [(i, (i + 1) % size) for i in range(size - 1)]
        down = [(j, i) for i, j in up]
        last = lax.slice_in_dim(shard, length - width, length, axis=dim)
        first = lax.slice_in_dim(shard, 0, width, axis=dim)
        before = lax.ppermute(last, axis, up)
        after = lax.ppermute(first, axis, down)
        shard = jnp.concatenate([before, shard, after], axis=dim)
    return shard


def passed_along(shard, axis, by):
    length = lax.axis_size(axis)
    pairs = [(i, i + by) for i in range(length) if 0 <= i + by < length]
    return lax.ppermute(shard, axis, pairs)


def flatten(block):
    return block.reshape(-1, block.shape[-1])


def product(left, right):
    return jnp.dot(flatten(left), right, preferred_element_type=jnp.float32)


def outer_sum(left, right):
    return lax.dot_general(
        flatten(left), flatten(right), (((0,), (0,)), ((), ())), preferred_element_type=jnp.float32
    )


def spatial_back(padded, kernel, height, width):
    total = None
    for i in range(3):
        for j in range(3):
            term = product(
                padded[:, :, 2 - i : 2 - i + height, 2 - j : 2 - j + width], kernel[i, j].T
            )
            total = term if total is None else total + term
    return total


def shards(frames_in, gain, spatial_w, temporal_w, cotangent):
    clips, frames, height, width, chans = frames_in.shape
    lead = (clips, frames, height, width, chans)
    upper = frames_in.astype(jnp.float32)
    recip = lax.rsqrt(jnp.mean(upper * upper, axis=-1, keepdims=True) + EPS)
    unit = upper * recip
    normed = (unit * gain).astype(jnp.bfloat16)
    banded = extended(normed, (("rows", 2),), 1)
    padded = jnp.pad(banded, ((0, 0), (0, 0), (0, 0), (1, 1), (0, 0)))
    hidden = None
    for i in range(3):
        for j in range(3):
            term = product(padded[:, :, i : i + height, j : j + width], spatial_w[i, j])
            hidden = term if hidden is None else hidden + term
    hidden = hidden.reshape(lead)
    act = jax.nn.silu(hidden).astype(jnp.bfloat16)
    earlier = passed_along(act, "tm", 1)
    act_pad = jnp.concatenate([earlier, act], axis=1)
    mixed = product(act_pad[:, 2 : 2 + frames], temporal_w[0])
    for k in range(1, 3):
        mixed = mixed + product(act_pad[:, 2 - k : 2 - k + frames], temporal_w[k])
    block_out = (upper + mixed.reshape(lead)).astype(jnp.bfloat16)
    later = passed_along(cotangent, "tm", -1)
    cot_pad = jnp.concatenate([cotangent, later], axis=1)
    dact = product(cot_pad[:, 0:frames], temporal_w[0].T)
    for k in range(1, 3):
        dact = dact + product(cot_pad[:, k : k + frames], temporal_w[k].T)
    sig = jax.nn.sigmoid(hidden)
    dhid = (dact.reshape(lead) * sig * (1.0 + hidden * (1.0 - sig))).astype(jnp.bfloat16)
    grad_temporal = jnp.stack(
        [outer_sum(act_pad[:, 2 - k : 2 - k + frames], cotangent) for k in range(3)]
    )
    cells_all = (
        clips
        * frames
        * height
        * width
        * lax.axis_size("rows")
        * lax.axis_size("tm")
        * lax.axis_size("dp")
    )
    scale = 1.0 / math.sqrt(cells_all)
    dzero = jnp.pad(dhid, ((0, 0), (0, 0), (2, 2), (1, 1), (0, 0)))
    whole = spatial_back(dzero, spatial_w, height + 2, width).reshape(
        (clips, frames, height + 2, width, chans)
    )
    from_above = passed_along(whole[:, :, height + 1 :].astype(jnp.bfloat16), "rows", 1).astype(
        jnp.float32
    )
    from_below = passed_along(whole[:, :, 0:1].astype(jnp.bfloat16), "rows", -1).astype(jnp.float32)
    dnorm = whole[:, :, 1 : height + 1]
    dnorm = dnorm.at[:, :, 0:1].add(from_above)
    dnorm = dnorm.at[:, :, height - 1 : height].add(from_below)
    spatial_rows = []
    for i in range(3):
        spatial_cols = []
        for j in range(3):
            spatial_cols.append(outer_sum(padded[:, :, i : i + height, j : j + width], dhid))
        spatial_rows.append(jnp.stack(spatial_cols))
    grad_spatial = jnp.stack(spatial_rows)
    grad_gain = jnp.sum(dnorm * unit, axis=(0, 1, 2, 3))
    grad_spatial, grad_temporal, grad_gain = lax.psum(
        (grad_spatial, grad_temporal, grad_gain), ("rows", "tm", "dp")
    )
    dunit = dnorm * gain
    grad_input = (
        cotangent.astype(jnp.float32)
        + recip * (dunit - unit * jnp.mean(dunit * unit, axis=-1, keepdims=True))
    ).astype(jnp.bfloat16)
    return (block_out, grad_input, grad_spatial * scale, grad_temporal * scale, grad_gain * scale)


def solution(mesh):
    return jax.shard_map(
        shards,
        mesh=mesh,
        in_specs=(
            P(("groups", "dp"), "tm", "rows", None, None),
            P(),
            P(),
            P(),
            P(("groups", "dp"), "tm", "rows", None, None),
        ),
        out_specs=(
            P(("groups", "dp"), "tm", "rows", None, None),
            P(("groups", "dp"), "tm", "rows", None, None),
            P("groups", None, None, None),
            P("groups", None, None),
            P("groups"),
        ),
        check_vma=False,
    )
```

profile of v0, /device:TPU:0, one launch (start us, length us, event | category | flops | bytes accessed | tf_op | source)
XLA Modules:
  0.0 192.7 jit_solution(13148399722400150449)
XLA Ops:
  7.2 1.6 fusion.13
  8.9 1.5 fusion.6
  10.4 4.9 %collective-permute-start = (bf16[1,2,1,320,128]{4,3,2,1,0:T(8,128)(2,1)S(1)}, bf16[1,2,1,320,128]{4,3,2,1,0:T(8,128)(2,1)S(1)}, u32[]{:S(2)}, u32[]{:S(2)}) collective-permute-start(bf16[1,2,1,320,128]{4,3,2,1,0:T(8,128)(2,1)S(1)} %get-tuple-element.58), channel_id=1, source_target_pairs={{0,4},{4,8},{8,12},{1,5},{5,9},{9,13},{2,6},{6,10},{10,14},{3,7},{... | collective-permute-start | bytes 491528 | tf_op jit(solution)/shard_map/ppermute | solution.py:17
  15.4 1.3 collective-permute-start.1
  16.7 1.3 collective-permute-start.3
  18.3 0.5 collective-permute-done
  18.8 4.1 %collective-permute-done.1 = bf16[1,2,1,320,128]{4,3,2,1,0:T(8,128)(2,1)S(1)} collective-permute-done((bf16[1,2,1,320,128]{4,3,2,1,0:T(8,128)(2,1)S(1)}, bf16[1,2,1,320,128]{4,3,2,1,0:T(8,128)(2,1)S(1)}, u32[]{:S(2)}, u32[]{:S(2)}) %collective-permute-start.1) | collective-permute-done | bytes 163872 | tf_op jit(solution)/shard_map/ppermute | solution.py:18
  23.2 0.8 fusion.95
  26.8 7.9 %collective-permute-done.3 = bf16[1,2,4,320,128]{4,3,2,1,0:T(8,128)(2,1)S(1)} collective-permute-done((bf16[1,2,4,320,128]{4,3,2,1,0:T(8,128)(2,1)S(1)}, bf16[1,2,4,320,128]{4,3,2,1,0:T(8,128)(2,1)S(1)}, u32[]{:S(2)}, u32[]{:S(2)}) %collective-permute-start.3) | collective-permute-done | bytes 655392 | tf_op jit(solution)/shard_map/ppermute | solution.py:26
  35.5 0.8 multiply_convert_fusion
  39.8 1.5 multiply_convert_fusion.1
  41.3 2.1 %pad_slice_fusion = (bf16[1,2,6,320,128]{4,3,2,1,0:T(8,128)(2,1)S(1)}, bf16[1,2,6,320,128]{4,3,2,1,0:T(8,128)(2,1)S(1)}, bf16[1,2,6,320,128]{4,3,2,1,0:T(8,128)(...) fusion(bf16[1,2,4,320,128]{4,3,2,1,0:T(8,128)(2,1)S(1)} %get-tu, ...), kind=kLoop, calls=%fused_computation.22 | loop fusion | bytes 9502720 | tf_op jit(solution)/shard_map/slice | solution.py:48
  43.8 0.4 convolution_add_fusion.7
  44.6 0.4 convolution_add_fusion.5
  45.5 0.4 convolution_add_fusion.3
  46.3 0.4 convolution_add_fusion.1
  47.4 1.5 collective-permute-start.2
  48.9 1.4 fusion.42
  50.3 1.3 collective-permute-start.5
  51.6 4.9 %collective-permute-start.4 = (bf16[1,2,1,320,128]{4,3,2,1,0:T(8,128)(2,1)S(1)}, bf16[1,2,1,320,128]{4,3,2,1,0:T(8,128)(2,1)S(1)}, u32[]{:S(2)}, u32[]{:S(2)}) collective-permute-start(bf16[1,2,1,320,128]{4,3,2,1,0:T(8,128)(2,1)S(1)} %get-tuple-element.44), channel_id=1, source_target_pairs={{0,4},{4,8},{8,12},{1,5},{5,9},{9,13},{2,6},{6,10},{10,14},{3,7},{... | collective-permute-start | bytes 491528 | tf_op jit(solution)/shard_map/ppermute | solution.py:26
  56.6 0.9 pad_maximum_fusion.4
  57.8 1.5 collective-permute-done.4
  59.5 0.9 fusion.12
  60.4 30.0 %psum.23 = f32[128]{0:T(128)S(1)} all-reduce(f32[128]{0:T(128)S(1)} %get-tuple-element.29), channel_id=1, replica_groups=mesh['groups'=2,'rows'=4,'tm'=2,'dp'=2] {'rows','tm','dp'}, use_global_device_ids=true, to_apply=%region_5.6 | all-reduce | flops 128 | bytes 1024 | tf_op jit(solution)/shard_map/psum | solution.py:115
  90.4 0.5 broadcast_multiply_fusion.3
  90.9 1.0 pad_maximum_fusion.1
  92.8 0.7 pad_maximum_fusion.5
  93.5 1.8 convolution_add_fusion.11
  95.7 1.6 fusion.11
  97.3 85.9 %all-reduce.5.cloned.1.call-done = (f32[3,3,128,128]{3,2,1,0:T(8,128)}, f32[3,128,128]{2,1,0:T(8,128)}) async-done(((f32[3,3,128,128]{3,2,1,0:T(8,128)}, f32[3,128,128]{2,1,0:T(8,128)}), (f32[3,3,128,128]{3,2,1,0:T(8,128)}, f32[3,128,128]{2,1,0:T(8,128)})) %all-reduce.5.cloned.1.call-update) | async-done | bytes 786448 | tf_op jit(solution)/shard_map/psum | solution.py:115
  183.2 2.0 %broadcast_multiply_fusion = f32[3,3,128,128]{3,2,1,0:T(8,128)} fusion(f32[3,3,128,128]{3,2,1,0:T(8,128)} %get-tuple-element.31), kind=kLoop, calls=%fused_computation.94 | loop fusion | flops 147456 | bytes 1179648 | tf_op jit(solution)/shard_map/mul | solution.py:123
  185.2 0.7 broadcast_multiply_fusion.1
  (60 shorter events, 11.5 us)
Async XLA Ops:
  7.2 9.5 %copy-start = (bf16[1,2,4,320,128]{4,3,2,1,0:T(8,128)(2,1)S(1)}, bf16[1,2,4,320,128]{4,3,2,1,0:T(8,128)(2,1)}, u32[]{:S(2)}) copy-start(bf16[1,2,4,320,128]{4,3,2,1,0:T(8,128)(2,1)} %param.13) | copy-start | bytes 1966084
  7.2 10.8 %copy-start.4 = (bf16[3,128,128]{2,1,0:T(8,128)(2,1)S(1)}, bf16[3,128,128]{2,1,0:T(8,128)(2,1)}, u32[]{:S(2)}) copy-start(bf16[3,128,128]{2,1,0:T(8,128)(2,1)} %param.12) | copy-start | bytes 294916
  7.2 176.0 %all-reduce.5.cloned.1.call-start = ((), (), s32[]{:S(2)}) async-start(), calls=%async_computation | async-start | bytes 1572864 | tf_op jit(solution)/shard_map/psum | solution.py:115
  10.4 8.4 %collective-permute-start = (bf16[1,2,1,320,128]{4,3,2,1,0:T(8,128)(2,1)S(1)}, bf16[1,2,1,320,128]{4,3,2,1,0:T(8,128)(2,1)S(1)}, u32[]{:S(2)}, u32[]{:S(2)}) collective-permute-start(bf16[1,2,1,320,128]{4,3,2,1,0:T(8,128)(2,1)S(1)} %get-tuple-element.58), channel_id=1, source_target_pairs={{0,4},{4,8},{8,12},{1,5},{5,9},{9,13},{2,6},{6,10},{10,14},{3,7},{... | collective-permute-start | bytes 491528 | tf_op jit(solution)/shard_map/ppermute | solution.py:17
  15.4 7.6 %collective-permute-start.1 = (bf16[1,2,1,320,128]{4,3,2,1,0:T(8,128)(2,1)S(1)}, bf16[1,2,1,320,128]{4,3,2,1,0:T(8,128)(2,1)S(1)}, u32[]{:S(2)}, u32[]{:S(2)}) collective-permute-start(bf16[1,2,1,320,128]{4,3,2,1,0:T(8,128)(2,1)S(1)} %get-tuple-element.59), channel_id=1, source_target_pairs={{4,0},{8,4},{12,8},{5,1},{9,5},{13,9},{6,2},{10,6},{14,10},{7,3},{... | collective-permute-start | bytes 491528 | tf_op jit(solution)/shard_map/ppermute | solution.py:18
  16.7 18.1 %collective-permute-start.3 = (bf16[1,2,4,320,128]{4,3,2,1,0:T(8,128)(2,1)S(1)}, bf16[1,2,4,320,128]{4,3,2,1,0:T(8,128)(2,1)S(1)}, u32[]{:S(2)}, u32[]{:S(2)}) collective-permute-start(bf16[1,2,4,320,128]{4,3,2,1,0:T(8,128)(2,1)S(1)} %copy-done), channel_id=1, source_target_pairs={{2,0},{3,1},{6,4},{7,5},{10,8},{11,9},{14,12},{15,13},{18,16},{19,... | collective-permute-start | bytes 1966088 | tf_op jit(solution)/shard_map/ppermute | solution.py:26
  23.2 1.0 copy-start.3
  47.4 43.5 %collective-permute-start.2 = (bf16[1,2,4,320,128]{4,3,2,1,0:T(8,128)(2,1)}, bf16[1,2,4,320,128]{4,3,2,1,0:T(8,128)(2,1)S(1)}, u32[]{:S(2)}, u32[]{:S(2)}) collective-permute-start(bf16[1,2,4,320,128]{4,3,2,1,0:T(8,128)(2,1)} %get-tuple-element.36), channel_id=1, source_target_pairs={{0,2},{1,3},{4,6},{5,7},{8,10},{9,11},{12,14},{13,15},{16,18},{17,... | collective-permute-start | bytes 1966088 | tf_op jit(solution)/shard_map/ppermute | solution.py:26
  50.3 9.1 %collective-permute-start.5 = (bf16[1,2,1,320,128]{4,3,2,1,0:T(8,128)(2,1)S(1)}, bf16[1,2,1,320,128]{4,3,2,1,0:T(8,128)(2,1)S(1)}, u32[]{:S(2)}, u32[]{:S(2)}) collective-permute-start(bf16[1,2,1,320,128]{4,3,2,1,0:T(8,128)(2,1)S(1)} %get-tuple-element.43), channel_id=1, source_target_pairs={{4,0},{8,4},{12,8},{5,1},{9,5},{13,9},{6,2},{10,6},{14,10},{7,3},{... | collective-permute-start | bytes 491528 | tf_op jit(solution)/shard_map/ppermute | solution.py:26
  51.6 7.7 %collective-permute-start.4 = (bf16[1,2,1,320,128]{4,3,2,1,0:T(8,128)(2,1)S(1)}, bf16[1,2,1,320,128]{4,3,2,1,0:T(8,128)(2,1)S(1)}, u32[]{:S(2)}, u32[]{:S(2)}) collective-permute-start(bf16[1,2,1,320,128]{4,3,2,1,0:T(8,128)(2,1)S(1)} %get-tuple-element.44), channel_id=1, source_target_pairs={{0,4},{4,8},{8,12},{1,5},{5,9},{9,13},{2,6},{6,10},{10,14},{3,7},{... | collective-permute-start | bytes 491528 | tf_op jit(solution)/shard_map/ppermute | solution.py:26
  57.5 2.0 %copy-start.1 = (bf16[1,2,4,320,128]{4,3,2,1,0:T(8,128)(2,1)S(1)}, bf16[1,2,4,320,128]{4,3,2,1,0:T(8,128)(2,1)}, u32[]{:S(2)}) copy-start(bf16[1,2,4,320,128]{4,3,2,1,0:T(8,128)(2,1)} %param.9) | copy-start | bytes 1966084
  57.5 2.0 %copy-start.6 = (f32[128]{0:T(128)S(1)}, f32[128]{0:T(128)}, u32[]{:S(2)}) copy-start(f32[128]{0:T(128)} %param.10) | copy-start | bytes 1540
  91.9 0.8 copy-start.2
  183.2 2.0 %copy-start.5 = (f32[3,128,128]{2,1,0:T(8,128)S(1)}, f32[3,128,128]{2,1,0:T(8,128)}, u32[]{:S(2)}) copy-start(f32[3,128,128]{2,1,0:T(8,128)} %get-tuple-element.32) | copy-start | bytes 589828
Sparse Core Ops, SparseCore 0:
  93.6 89.5 all-reduce.4
where the time goes:
time: 193 us
  waiting for transfers between devices  100 us (52%)
  blocking collectives  30 us (16%)
  matrix products  16.1 us (8%)
  starting transfers between devices  15.3 us (8%)
  between operations  14.4 us (7%)
  other arithmetic  13.6 us (7%)
  local copies, waits for them, and re-layouts  3.27 us (2%)
    psum x1, waiting for transfers between devices, shards(): lax.psum((grad_spatial, grad_temporal, grad_gain), ('rows', 'tm', 'dp'))  85.9 us
    psum x1, blocking collectives, shards(): lax.psum((grad_spatial, grad_temporal, grad_gain), ('rows', 'tm', 'dp'))  30 us
    dot_general x24, matrix products, product(): return jnp.dot(flatten(left), right, preferred_element_type=jnp.float32)  11.6 us
    ppermute x4, waiting for transfers between devices, passed_along(): return lax.ppermute(shard, axis, pairs)  9.45 us
    ppermute x4, starting transfers between devices, passed_along(): return lax.ppermute(shard, axis, pairs)  8.98 us
    ppermute x1, starting transfers between devices, extended(): before = lax.ppermute(last, axis, up)  4.94 us
    dot_general x12, matrix products, outer_sum(): lax.dot_general(flatten(left), flatten(right), (((0,), (0,)), ((), ())),...  4.54 us
    ppermute x1, waiting for transfers between devices, extended(): after = lax.ppermute(first, axis, down)  4.12 us
  transfers between devices with their start and end apart: 7, of which 5 were waited for; matrix products, arithmetic and copies ran while one was open for 6% of the time, Pallas kernels for 0%

commit v1 on v0

--- a/solution.py
+++ b/solution.py
@@ -113,7 +113,7 @@
     grad_spatial = jnp.stack(spatial_rows)
     grad_gain = jnp.sum(dnorm * unit, axis=(0, 1, 2, 3))
     grad_spatial, grad_temporal, grad_gain = lax.psum(
-        (grad_spatial, grad_temporal, grad_gain), ("rows", "tm", "dp")
+        lax.psum((grad_spatial, grad_temporal, grad_gain), ("tm", "dp")), "rows"
     )
     dunit = dnorm * gain
     grad_input = (

time: 193 us -> 171 us (0.89)
  waiting for transfers between devices: 100 us -> 88.6 us
  blocking collectives: 30 us -> 19.1 us
    psum x1 -> x2, waiting for transfers between devices: 85.9 us -> 74.5 us  [the longest x1 42.7 us: shards(): lax.psum(lax.psum((grad_spatial, grad_temporal, grad_gain), ('tm', 'dp'))...]
    psum x1 -> x2, blocking collectives: 30 us -> 19.1 us  [the longest x1 13.3 us: shards(): lax.psum(lax.psum((grad_spatial, grad_temporal, grad_gain), ('tm', 'dp'))...]
  transfers between devices with their start and end apart: 7 -> 8, of which waited for: 5 -> 6; matrix products, arithmetic and copies ran while one was open for 6% -> 7% of each run, Pallas kernels for 0% -> 0%
where the time goes in v1:
time: 171 us; the launch traced here: 170 us
  waiting for transfers between devices  88.6 us (52%)
  blocking collectives  19.1 us (11%)
  matrix products  16.1 us (9%)
  starting transfers between devices  15.3 us (9%)
  between operations  14.5 us (8%)
  other arithmetic  13.6 us (8%)
  local copies, waits for them, and re-layouts  3.27 us (2%)
    psum x1, waiting for transfers between devices, shards(): lax.psum(lax.psum((grad_spatial, grad_temporal, grad_gain), ('tm', 'dp'))...  42.7 us
    psum x1, waiting for transfers between devices, shards(): lax.psum((grad_spatial, grad_temporal, grad_gain), ('tm', 'dp'))  31.8 us
    psum x1, blocking collectives, shards(): lax.psum(lax.psum((grad_spatial, grad_temporal, grad_gain), ('tm', 'dp'))...  13.3 us
    dot_general x24, matrix products, product(): return jnp.dot(flatten(left), right, preferred_element_type=jnp.float32)  11.6 us
    ppermute x4, waiting for transfers between devices, passed_along(): return lax.ppermute(shard, axis, pairs)  9.45 us
    ppermute x4, starting transfers between devices, passed_along(): return lax.ppermute(shard, axis, pairs)  8.98 us
    psum x1, blocking collectives, shards(): lax.psum((grad_spatial, grad_temporal, grad_gain), ('tm', 'dp'))  5.76 us
    ppermute x1, starting transfers between devices, extended(): before = lax.ppermute(last, axis, up)  4.94 us
  transfers between devices with their start and end apart: 8, of which 6 were waited for; matrix products, arithmetic and copies ran while one was open for 7% of the time, Pallas kernels for 0%

profile of v1, /device:TPU:0, one launch (start us, length us, event | category | flops | bytes accessed | tf_op | source)
XLA Modules:
  0.0 170.4 jit_solution(6987809129392744511)
XLA Ops:
  7.2 1.6 fusion.13
  8.9 1.5 fusion.6
  10.4 4.9 %collective-permute-start = (bf16[1,2,1,320,128]{4,3,2,1,0:T(8,128)(2,1)S(1)}, bf16[1,2,1,320,128]{4,3,2,1,0:T(8,128)(2,1)S(1)}, u32[]{:S(2)}, u32[]{:S(2)}) collective-permute-start(bf16[1,2,1,320,128]{4,3,2,1,0:T(8,128)(2,1)S(1)} %get-tuple-element.60), channel_id=1, source_target_pairs={{0,4},{4,8},{8,12},{1,5},{5,9},{9,13},{2,6},{6,10},{10,14},{3,7},{... | collective-permute-start | bytes 491528 | tf_op jit(solution)/shard_map/ppermute | solution.py:17
  15.4 1.3 collective-permute-start.1
  16.7 1.3 collective-permute-start.3
  18.3 0.5 collective-permute-done
  18.8 4.1 %collective-permute-done.1 = bf16[1,2,1,320,128]{4,3,2,1,0:T(8,128)(2,1)S(1)} collective-permute-done((bf16[1,2,1,320,128]{4,3,2,1,0:T(8,128)(2,1)S(1)}, bf16[1,2,1,320,128]{4,3,2,1,0:T(8,128)(2,1)S(1)}, u32[]{:S(2)}, u32[]{:S(2)}) %collective-permute-start.1) | collective-permute-done | bytes 163872 | tf_op jit(solution)/shard_map/ppermute | solution.py:18
  23.2 0.8 fusion.95
  26.8 7.9 %collective-permute-done.3 = bf16[1,2,4,320,128]{4,3,2,1,0:T(8,128)(2,1)S(1)} collective-permute-done((bf16[1,2,4,320,128]{4,3,2,1,0:T(8,128)(2,1)S(1)}, bf16[1,2,4,320,128]{4,3,2,1,0:T(8,128)(2,1)S(1)}, u32[]{:S(2)}, u32[]{:S(2)}) %collective-permute-start.3) | collective-permute-done | bytes 655392 | tf_op jit(solution)/shard_map/ppermute | solution.py:26
  35.5 0.8 multiply_convert_fusion
  39.8 1.5 multiply_convert_fusion.1
  41.3 2.1 %pad_slice_fusion = (bf16[1,2,6,320,128]{4,3,2,1,0:T(8,128)(2,1)S(1)}, bf16[1,2,6,320,128]{4,3,2,1,0:T(8,128)(2,1)S(1)}, bf16[1,2,6,320,128]{4,3,2,1,0:T(8,128)(...) fusion(bf16[1,2,4,320,128]{4,3,2,1,0:T(8,128)(2,1)S(1)} %get-tu, ...), kind=kLoop, calls=%fused_computation.22 | loop fusion | bytes 9502720 | tf_op jit(solution)/shard_map/slice | solution.py:48
  45.5 0.4 convolution_add_fusion.3
  46.3 0.4 convolution_add_fusion.1
  47.4 1.5 collective-permute-start.2
  48.9 1.4 fusion.42
  50.3 1.3 collective-permute-start.5
  51.6 4.9 %collective-permute-start.4 = (bf16[1,2,1,320,128]{4,3,2,1,0:T(8,128)(2,1)S(1)}, bf16[1,2,1,320,128]{4,3,2,1,0:T(8,128)(2,1)S(1)}, u32[]{:S(2)}, u32[]{:S(2)}) collective-permute-start(bf16[1,2,1,320,128]{4,3,2,1,0:T(8,128)(2,1)S(1)} %get-tuple-element.46), channel_id=1, source_target_pairs={{0,4},{4,8},{8,12},{1,5},{5,9},{9,13},{2,6},{6,10},{10,14},{3,7},{... | collective-permute-start | bytes 491528 | tf_op jit(solution)/shard_map/ppermute | solution.py:26
  56.6 0.9 pad_maximum_fusion.4
  57.8 1.5 collective-permute-done.4
  59.5 0.9 fusion.12
  60.4 5.8 %psum.46 = f32[128]{0:T(128)S(1)} all-reduce(f32[128]{0:T(128)S(1)} %get-tuple-element.29), channel_id=1, replica_groups=mesh['groups'=2,'rows'=4,'tm'=2,'dp'=2] {'tm','dp'}, use_global_device_ids=true, to_apply=%region_7.8 | all-reduce | flops 128 | bytes 1024 | tf_op jit(solution)/shard_map/psum | solution.py:116
  66.1 13.3 %psum.47 = f32[128]{0:T(128)S(1)} all-reduce(f32[128]{0:T(128)S(1)} %psum.46), channel_id=1, replica_groups=mesh['groups'=2,'rows'=4,'tm'=2,'dp'=2] {'rows'}, use_global_device_ids=true, to_apply=%region_8.9 | all-reduce | flops 128 | bytes 1024 | tf_op jit(solution)/shard_map/psum | solution.py:115
  79.4 1.0 pad_maximum_fusion.1
  81.3 0.7 pad_maximum_fusion.5
  82.1 0.5 broadcast_multiply_fusion.3
  82.6 31.8 %all-reduce.7.cloned.1.call-done = (f32[3,3,128,128]{3,2,1,0:T(8,128)}, f32[3,128,128]{2,1,0:T(8,128)}) async-done(((f32[3,3,128,128]{3,2,1,0:T(8,128)}, f32[3,128,128]{2,1,0:T(8,128)}), (f32[3,3,128,128]{3,2,1,0:T(8,128)}, f32[3,128,128]{2,1,0:T(8,128)})) %all-reduce.7.cloned.1.call-update) | async-done | bytes 786448 | tf_op jit(solution)/shard_map/psum | solution.py:116
  114.4 1.8 %convolution_add_fusion.11 = f32[2560,128]{1,0:T(8,128)S(1)} fusion(f32[2560,128]{1,0:T(8,128)} %fusion.42, bf16[2560,128]{1,0:T(8,128)(2,1)} %bitcast.249, bf16[3,128,128]{2,1,0:T(8,128)(2,1)S(1)} %copy-done.4), kind=kOutput, calls=%fused_computation.11 | convolution fusion | flops 84213760 | bytes 3309568 | tf_op jit(solution)/shard_map/dot_general | solution.py:34
  116.6 1.6 fusion.11
  118.2 42.7 %all-reduce.9.cloned.1.call-done = (f32[3,3,128,128]{3,2,1,0:T(8,128)}, f32[3,128,128]{2,1,0:T(8,128)}) async-done(((f32[3,3,128,128]{3,2,1,0:T(8,128)}, f32[3,128,128]{2,1,0:T(8,128)}), (f32[3,3,128,128]{3,2,1,0:T(8,128)}, f32[3,128,128]{2,1,0:T(8,128)})) %all-reduce.9.cloned.1.call-update) | async-done | bytes 786448 | tf_op jit(solution)/shard_map/psum | solution.py:115
  160.9 2.0 %broadcast_multiply_fusion = f32[3,3,128,128]{3,2,1,0:T(8,128)} fusion(f32[3,3,128,128]{3,2,1,0:T(8,128)} %get-tuple-element.33), kind=kLoop, calls=%fused_computation.94 | loop fusion | flops 147456 | bytes 1179648 | tf_op jit(solution)/shard_map/mul | solution.py:123
  162.9 0.7 broadcast_multiply_fusion.1
  (64 shorter events, 12.4 us)
Async XLA Ops:
  7.2 9.5 %copy-start = (bf16[1,2,4,320,128]{4,3,2,1,0:T(8,128)(2,1)S(1)}, bf16[1,2,4,320,128]{4,3,2,1,0:T(8,128)(2,1)}, u32[]{:S(2)}) copy-start(bf16[1,2,4,320,128]{4,3,2,1,0:T(8,128)(2,1)} %param.13) | copy-start | bytes 1966084
  7.2 10.8 %copy-start.4 = (bf16[3,128,128]{2,1,0:T(8,128)(2,1)S(1)}, bf16[3,128,128]{2,1,0:T(8,128)(2,1)}, u32[]{:S(2)}) copy-start(bf16[3,128,128]{2,1,0:T(8,128)(2,1)} %param.12) | copy-start | bytes 294916
  7.2 107.2 %all-reduce.7.cloned.1.call-start = ((), (), s32[]{:S(2)}) async-start(), calls=%async_computation | async-start | bytes 1572864 | tf_op jit(solution)/shard_map/psum | solution.py:116
  10.4 8.4 %collective-permute-start = (bf16[1,2,1,320,128]{4,3,2,1,0:T(8,128)(2,1)S(1)}, bf16[1,2,1,320,128]{4,3,2,1,0:T(8,128)(2,1)S(1)}, u32[]{:S(2)}, u32[]{:S(2)}) collective-permute-start(bf16[1,2,1,320,128]{4,3,2,1,0:T(8,128)(2,1)S(1)} %get-tuple-element.60), channel_id=1, source_target_pairs={{0,4},{4,8},{8,12},{1,5},{5,9},{9,13},{2,6},{6,10},{10,14},{3,7},{... | collective-permute-start | bytes 491528 | tf_op jit(solution)/shard_map/ppermute | solution.py:17
  15.4 7.6 %collective-permute-start.1 = (bf16[1,2,1,320,128]{4,3,2,1,0:T(8,128)(2,1)S(1)}, bf16[1,2,1,320,128]{4,3,2,1,0:T(8,128)(2,1)S(1)}, u32[]{:S(2)}, u32[]{:S(2)}) collective-permute-start(bf16[1,2,1,320,128]{4,3,2,1,0:T(8,128)(2,1)S(1)} %get-tuple-element.61), channel_id=1, source_target_pairs={{4,0},{8,4},{12,8},{5,1},{9,5},{13,9},{6,2},{10,6},{14,10},{7,3},{... | collective-permute-start | bytes 491528 | tf_op jit(solution)/shard_map/ppermute | solution.py:18
  16.7 18.1 %collective-permute-start.3 = (bf16[1,2,4,320,128]{4,3,2,1,0:T(8,128)(2,1)S(1)}, bf16[1,2,4,320,128]{4,3,2,1,0:T(8,128)(2,1)S(1)}, u32[]{:S(2)}, u32[]{:S(2)}) collective-permute-start(bf16[1,2,4,320,128]{4,3,2,1,0:T(8,128)(2,1)S(1)} %copy-done), channel_id=1, source_target_pairs={{2,0},{3,1},{6,4},{7,5},{10,8},{11,9},{14,12},{15,13},{18,16},{19,... | collective-permute-start | bytes 1966088 | tf_op jit(solution)/shard_map/ppermute | solution.py:26
  23.2 1.0 copy-start.3
  47.4 32.0 %collective-permute-start.2 = (bf16[1,2,4,320,128]{4,3,2,1,0:T(8,128)(2,1)}, bf16[1,2,4,320,128]{4,3,2,1,0:T(8,128)(2,1)S(1)}, u32[]{:S(2)}, u32[]{:S(2)}) collective-permute-start(bf16[1,2,4,320,128]{4,3,2,1,0:T(8,128)(2,1)} %get-tuple-element.38), channel_id=1, source_target_pairs={{0,2},{1,3},{4,6},{5,7},{8,10},{9,11},{12,14},{13,15},{16,18},{17,... | collective-permute-start | bytes 1966088 | tf_op jit(solution)/shard_map/ppermute | solution.py:26
  50.3 9.1 %collective-permute-start.5 = (bf16[1,2,1,320,128]{4,3,2,1,0:T(8,128)(2,1)S(1)}, bf16[1,2,1,320,128]{4,3,2,1,0:T(8,128)(2,1)S(1)}, u32[]{:S(2)}, u32[]{:S(2)}) collective-permute-start(bf16[1,2,1,320,128]{4,3,2,1,0:T(8,128)(2,1)S(1)} %get-tuple-element.45), channel_id=1, source_target_pairs={{4,0},{8,4},{12,8},{5,1},{9,5},{13,9},{6,2},{10,6},{14,10},{7,3},{... | collective-permute-start | bytes 491528 | tf_op jit(solution)/shard_map/ppermute | solution.py:26
  51.6 7.7 %collective-permute-start.4 = (bf16[1,2,1,320,128]{4,3,2,1,0:T(8,128)(2,1)S(1)}, bf16[1,2,1,320,128]{4,3,2,1,0:T(8,128)(2,1)S(1)}, u32[]{:S(2)}, u32[]{:S(2)}) collective-permute-start(bf16[1,2,1,320,128]{4,3,2,1,0:T(8,128)(2,1)S(1)} %get-tuple-element.46), channel_id=1, source_target_pairs={{0,4},{4,8},{8,12},{1,5},{5,9},{9,13},{2,6},{6,10},{10,14},{3,7},{... | collective-permute-start | bytes 491528 | tf_op jit(solution)/shard_map/ppermute | solution.py:26
  57.5 2.0 %copy-start.1 = (bf16[1,2,4,320,128]{4,3,2,1,0:T(8,128)(2,1)S(1)}, bf16[1,2,4,320,128]{4,3,2,1,0:T(8,128)(2,1)}, u32[]{:S(2)}) copy-start(bf16[1,2,4,320,128]{4,3,2,1,0:T(8,128)(2,1)} %param.9) | copy-start | bytes 1966084
  57.5 2.0 %copy-start.6 = (f32[128]{0:T(128)S(1)}, f32[128]{0:T(128)}, u32[]{:S(2)}) copy-start(f32[128]{0:T(128)} %param.10) | copy-start | bytes 1540
  80.4 0.8 copy-start.2
  82.0 78.9 %all-reduce.9.cloned.1.call-start = ((), (), s32[]{:S(2)}) async-start(), calls=%async_computation.1 | async-start | bytes 1572864 | tf_op jit(solution)/shard_map/psum | solution.py:115
  160.9 2.0 %copy-start.5 = (f32[3,128,128]{2,1,0:T(8,128)S(1)}, f32[3,128,128]{2,1,0:T(8,128)}, u32[]{:S(2)}) copy-start(f32[3,128,128]{2,1,0:T(8,128)} %get-tuple-element.34) | copy-start | bytes 589828
Sparse Core Ops, SparseCore 0:
  82.1 32.2 all-reduce.6
  116.8 44.0 all-reduce.8
